TPU v7x, 256 devices: a whole 4x4x8 slice. The times are simulated.
256 devices in a mesh: leaf: 32 (over x, z), near: 8 (over y, core).
Axes of the slice: x: 4, y: 4, z: 8, core: 2. Of those that a mesh axis runs over, the one named last changes fastest.
Arguments:
- charges: bfloat16 [2048, 16, 128], P(('leaf', 'near')), may hold values from -6 to 6
- leaf_in: bfloat16 [2048, 64, 128], P(('leaf', 'near')), may hold values from -0.5 to 0.5
- leaf_out: bfloat16 [2048, 64, 128], P(('leaf', 'near')), may hold values from -0.75 to 0.75
- near_list: int32 [2048, 27], P(('leaf', 'near')), may hold values from 0 to 2047, as said below
- near_blocks: bfloat16 [2048, 27, 128, 128], P(('leaf', 'near')), may hold values from -0.109375 to 0.109375
- leaf_partners: int32 [2048, 8], P(('leaf', 'near')), may hold values from 0 to 2047, as said below
- leaf_couple: bfloat16 [2048, 64, 512], P(('leaf', 'near')), may hold values from -0.25 to 0.25
- leaf_up: bfloat16 [256, 64, 512], P(('leaf', 'near')), may hold values from -0.25 to 0.25
- leaf_down: bfloat16 [256, 64, 512], P(('leaf', 'near')), may hold values from -0.75 to 0.75
- box_partners: int32 [256, 8], P(('leaf', 'near')), may hold values from 0 to 255, as said below
- box_couple: bfloat16 [256, 64, 512], P(('leaf', 'near')), may hold values from -0.25 to 0.25
- box_transfer: bfloat16 [256, 64, 128], P(('leaf', 'near')), may hold values from -0.25 to 0.25
- top_partners: int32 [32, 8], P('leaf'), may hold values from 0 to 31
- top_couple: bfloat16 [32, 64, 512], P('leaf'), may hold values from -0.25 to 0.25
Outputs:
- potential: bfloat16 [2048, 16, 128], P(('leaf', 'near'))
Inputs may be any that keep to these rules, and one draw needn't show every extreme that they name: `near_list`: leaves are numbered subtree by subtree, 8 to a device box and 8 device boxes to a subtree. Entry [l, s] names a leaf of the subtree of leaf l, or a leaf of the device box at the same place as l's box in the subtree just before or just after l's. Entries may repeat. `leaf_partners`: entry [l, c] names a leaf of the subtree of leaf l, or a leaf of the device box at the same place as l's box in the subtree just before or just after l's. Entries may repeat. `box_partners`: entry [b, c] names a device box of the subtree of box b. Entries may repeat.
All inputs are finite; a program needn't handle non-finite values.
Results may differ from a plain program's by a relative error of at most 0.015.
Values may be sent and summed in bfloat16 or wider, within the bound.
A program may use at most 64 MiB of HBM per device.

v0:
```python
import jax
import jax.numpy as jnp
from jax import lax
from jax.sharding import PartitionSpec as P


def padded(cells, sides, width):
    for axis, dim in sides:
        count = lax.axis_size(axis)
        ends = count - 1
        head = lax.slice_in_dim(cells, 0, width, axis=dim)
        tail = lax.slice_in_dim(cells, cells.shape[dim] - width, cells.shape[dim], axis=dim)
        cells = jnp.concatenate(
            [
                lax.ppermute(tail, axis, [(i, (i + 1) % count) for i in range(ends)]),
                cells,
                lax.ppermute(head, axis, [((i + 1) % count, i) for i in range(ends)]),
            ],
            axis=dim,
        )
    return cells


def side_by_side(table, partners, rhs_count, rank_width):
    picked = table[partners].reshape(partners.shape[0], rhs_count, rank_width)
    return picked.transpose(1, 0, 2).reshape(rhs_count, partners.shape[0] * rank_width)


def per_device(
    charges,
    leaf_in,
    leaf_out,
    near_list,
    near_blocks,
    leaf_partners,
    leaf_couple,
    leaf_up,
    leaf_down,
    box_partners,
    box_couple,
    box_transfer,
    top_partners,
    top_couple,
):
    leaf_count = charges.shape[0]
    rhs_count = charges.shape[1]
    point_count = charges.shape[2]
    rank_width = leaf_in.shape[1]
    near_size = lax.axis_size("near")
    subtree = lax.axis_index("leaf")
    position = lax.axis_index("near")
    group_len = leaf_count * near_size
    charge_width = rhs_count * point_count
    moments = jnp.einsum(
        "lrp,lkp->lrk", charges, leaf_in, preferred_element_type=jnp.float32
    ).astype(jnp.bfloat16)
    flat_rows = jnp.concatenate(
        [
            charges.reshape(leaf_count, charge_width),
            moments.reshape(leaf_count, rhs_count * rank_width),
        ],
        axis=1,
    )
    group_rows = lax.all_gather(flat_rows, "near", axis=0, tiled=True)
    rim_rows = padded(flat_rows, (("leaf", 0),), leaf_count)
    window = jnp.concatenate(
        [group_rows, rim_rows[:leaf_count], rim_rows[2 * leaf_count :]], axis=0
    )
    window_charges = window[:, :charge_width].reshape(-1, rhs_count, point_count)
    window_moments = window[:, charge_width:].reshape(-1, rhs_count, rank_width)
    own_start = subtree * group_len
    lower_start = (subtree - 1) * group_len + position * leaf_count
    upper_start = (subtree + 1) * group_len + position * leaf_count

    def locate(leaf_ids):
        inside = (leaf_ids >= own_start) & (leaf_ids < own_start + group_len)
        outside = jnp.where(
            leaf_ids < own_start,
            group_len + leaf_ids - lower_start,
            group_len + leaf_count + leaf_ids - upper_start,
        )
        return jnp.where(inside, leaf_ids - own_start, outside)

    stacked = moments.transpose(1, 0, 2).reshape(rhs_count, leaf_count * rank_width)
    box_moment = jnp.einsum(
        "ri,oi->ro", stacked, leaf_up[0], preferred_element_type=jnp.float32
    ).astype(jnp.bfloat16)
    share_row = jnp.dot(
        box_moment, box_transfer[0][:, :rank_width], preferred_element_type=jnp.float32
    ).astype(jnp.bfloat16)
    flat_box = box_moment.reshape(1, rhs_count * rank_width)
    flat_share = share_row.reshape(1, rhs_count * rank_width)
    all_boxes, all_shares = (
        lax.all_gather(flat_box, ("leaf", "near"), axis=0, tiled=True),
        lax.all_gather(flat_share, ("leaf", "near"), axis=0, tiled=True),
    )
    subtree_count = lax.axis_size("leaf")
    top_moments = (
        all_shares.astype(jnp.float32)
        .reshape(subtree_count, near_size, rhs_count * rank_width)
        .sum(axis=1)
        .astype(jnp.bfloat16)
    )
    group_boxes = lax.dynamic_slice_in_dim(all_boxes, subtree * near_size, near_size, 0)
    top_in = side_by_side(top_moments, top_partners[0], rhs_count, rank_width)
    top_local = jnp.einsum(
        "ri,oi->ro", top_in, top_couple[0], preferred_element_type=jnp.float32
    ).astype(jnp.bfloat16)
    box_in = side_by_side(group_boxes, box_partners[0] - subtree * near_size, rhs_count, rank_width)
    box_local = jnp.einsum("ri,oi->ro", box_in, box_couple[0], preferred_element_type=jnp.float32)
    box_local = (
        box_local
        + jnp.dot(top_local, box_transfer[0][:, rank_width:], preferred_element_type=jnp.float32)
    ).astype(jnp.bfloat16)
    gathered = window_charges[locate(near_list)]
    near_field = jnp.einsum(
        "lsrp,lspq->lrq", gathered, near_blocks, preferred_element_type=jnp.float32
    )
    partner_moments = window_moments[locate(leaf_partners)]
    partner_moments = partner_moments.transpose(0, 2, 1, 3).reshape(leaf_count, rhs_count, -1)
    coupled = jnp.einsum(
        "lri,loi->lro", partner_moments, leaf_couple, preferred_element_type=jnp.float32
    )
    from_box = jnp.dot(box_local, leaf_down[0], preferred_element_type=jnp.float32)
    from_box = from_box.reshape(rhs_count, leaf_count, rank_width).transpose(1, 0, 2)
    leaf_local = (coupled + from_box).astype(jnp.bfloat16)
    far_field = jnp.einsum("lrk,lkq->lrq", leaf_local, leaf_out, preferred_element_type=jnp.float32)
    return (near_field + far_field).astype(jnp.bfloat16)


def solution(mesh):
    return jax.shard_map(
        per_device,
        mesh=mesh,
        in_specs=(
            P(("leaf", "near"), None, None),
            P(("leaf", "near"), None, None),
            P(("leaf", "near"), None, None),
            P(("leaf", "near"), None),
            P(("leaf", "near"), None, None, None),
            P(("leaf", "near"), None),
            P(("leaf", "near"), None, None),
            P(("leaf", "near"), None, None),
            P(("leaf", "near"), None, None),
            P(("leaf", "near"), None),
            P(("leaf", "near"), None, None),
            P(("leaf", "near"), None, None),
            P("leaf", None),
            P("leaf", None, None),
        ),
        out_specs=P(("leaf", "near"), None, None),
        check_vma=False,
    )
```

profile of v0, /device:TPU:1, one launch (start us, length us, event | category | flops | bytes accessed | tf_op | source)
XLA Modules:
  0.0 168.3 jit_solution(3950723500973915505)
XLA Ops:
  0.0 1.1 convolution_convert_fusion
  1.3 0.8 bitcast_dynamic-update-slice_fusion
  2.0 1.3 collective-permute-start.1
  3.3 5.0 %collective-permute-start = (bf16[8,3072]{1,0:T(8,128)(2,1)S(1)}, bf16[8,3072]{1,0:T(8,128)(2,1)S(1)}, u32[]{:S(2)}, u32[]{:S(2)}) collective-permute-start(bf16[8,3072]{1,0:T(8,128)(2,1)S(1)} %constant_dynamic-update-slice_fusion), channel_id=1, source_target_pairs={{0,8},{8,16},{16,24},{24,32},{32,40},{40,48},{48,56},{56,64},{64,7... | collective-permute-start | bytes 147464 | tf_op jit(solution)/shard_map/ppermute | solution.py:15
  8.4 15.6 %all_gather.9 = bf16[64,3072]{1,0:T(8,128)(2,1)S(1)} all-gather(bf16[8,3072]{1,0:T(8,128)(2,1)S(1)} %constant_dynamic-update-slice_fusion), channel_id=1, replica_groups=mesh['leaf'=32,'near'=8] {'near'}, dimensions={0}, use_global_device_ids=true | all-gather | bytes 442368 | tf_op jit(solution)/shard_map/all_gather | solution.py:64
  24.0 0.7 fusion.12
  24.6 0.7 fusion.13
  25.3 0.7 compare_select_fusion.1
  26.1 0.7 compare_select_fusion
  27.0 1.0 convolution_convert_fusion.3
  28.0 0.8 convolution_convert_fusion.2
  29.0 66.6 %all-gather.1 = bf16[256,1,1024]{2,1,0:T(2,128)(2,1)S(1)} all-gather(bf16[1,1,1024]{2,1,0:T(2,128)(2,1)S(1)} %reshape.145), channel_id=1, replica_groups=mesh['leaf'=32,'near'=8] {'leaf','near'}, dimensions={0}, use_global_device_ids=true | all-gather | bytes 526336 | tf_op jit(solution)/shard_map/all_gather | solution.py:95
  95.5 0.4 bitcast_reduce_fusion
  96.0 0.6 gather_fusion.3
  96.8 60.2 %all-gather = bf16[256,1,1024]{2,1,0:T(2,128)(2,1)S(1)} all-gather(bf16[1,1,1024]{2,1,0:T(2,128)(2,1)S(1)} %reshape.143), channel_id=1, replica_groups=mesh['leaf'=32,'near'=8] {'leaf','near'}, dimensions={0}, use_global_device_ids=true | all-gather | bytes 526336 | tf_op jit(solution)/shard_map/all_gather | solution.py:94
  157.1 0.6 gather_fusion.2
  157.9 1.0 fusion.7
  158.8 1.1 fusion.4
  159.9 1.0 copy.28
  161.3 0.6 gather_fusion.1
  162.2 0.2 fusion.14
  162.5 0.8 gather_fusion
  163.3 4.1 %convolution_bitcast_fusion.1 = f32[8,16,128]{2,1,0:T(8,128)S(1)} fusion(bf16[8,27,16,128]{3,2,1,0:T(8,128)(2,1)S(1)} %bitcast.75, bf16[8,27,128,128]{3,2,1,0:T(8,128)(2,1)} %param.18), kind=kOutput, calls=%fused_computation.7 | convolution fusion | flops 113246208 | bytes 8028160 | tf_op jit(solution)/shard_map/lsrp,lspq->lrq/dot_general | solution.py:116
  167.4 1.0 fusion.2
  (34 shorter events, 1.7 us)
Async XLA Ops:
  0.0 162.2 %copy-start = (bf16[8,64,512]{2,1,0:T(8,128)(2,1)S(1)}, bf16[8,64,512]{2,1,0:T(8,128)(2,1)}, u32[]{:S(2)}) copy-start(bf16[8,64,512]{2,1,0:T(8,128)(2,1)} %param.20) | copy-start | bytes 1572868
  2.0 158.9 %collective-permute-start.1 = (bf16[8,3072]{1,0:T(8,128)(2,1)S(1)}, bf16[8,3072]{1,0:T(8,128)(2,1)S(1)}, u32[]{:S(2)}, u32[]{:S(2)}) collective-permute-start(bf16[8,3072]{1,0:T(8,128)(2,1)S(1)} %constant_dynamic-update-slice_fusion), channel_id=1, source_target_pairs={{8,0},{16,8},{24,16},{32,24},{40,32},{48,40},{56,48},{64,56},{72,6... | collective-permute-start | bytes 147464 | tf_op jit(solution)/shard_map/ppermute | solution.py:17
  3.3 157.5 %collective-permute-start = (bf16[8,3072]{1,0:T(8,128)(2,1)S(1)}, bf16[8,3072]{1,0:T(8,128)(2,1)S(1)}, u32[]{:S(2)}, u32[]{:S(2)}) collective-permute-start(bf16[8,3072]{1,0:T(8,128)(2,1)S(1)} %constant_dynamic-update-slice_fusion), channel_id=1, source_target_pairs={{0,8},{8,16},{16,24},{24,32},{32,40},{40,48},{48,56},{56,64},{64,7... | collective-permute-start | bytes 147464 | tf_op jit(solution)/shard_map/ppermute | solution.py:15
  161.0 6.4 %copy-start.1 = (bf16[8,64,128]{2,1,0:T(8,128)(2,1)S(1)}, bf16[8,64,128]{2,1,0:T(8,128)(2,1)}, u32[]{:S(2)}) copy-start(bf16[8,64,128]{2,1,0:T(8,128)(2,1)} %param.16) | copy-start | bytes 393220
where the time goes:
time: 169 us; the launch traced here: 168 us
  blocking collectives  142 us (84%)
  matrix products  10.3 us (6%)
  starting transfers between devices  6.29 us (4%)
  local copies, waits for them, and re-layouts  6.02 us (4%)
  other arithmetic  3.16 us (2%)
    all_gather x1, blocking collectives, per_device(): lax.all_gather(flat_share, ('leaf', 'near'), axis=0, tiled=True)  66.6 us
    all_gather x1, blocking collectives, per_device(): lax.all_gather(flat_box, ('leaf', 'near'), axis=0, tiled=True)  60.2 us
    all_gather x1, blocking collectives, per_device(): group_rows = lax.all_gather(flat_rows, 'near', axis=0, tiled=True)  15.6 us
    ppermute x1, starting transfers between devices, padded(): lax.ppermute(tail, axis, [(i, (i + 1) % count) for i in range(ends)])  5 us
    dot_general x1, matrix products, per_device(): jnp.einsum('lsrp,lspq->lrq', gathered, near_blocks, preferred_element_typ...  4.07 us
  transfers between devices with their start and end apart: 2, of which 0 were waited for; matrix products, arithmetic and copies ran while one was open for 6% of the time, Pallas kernels for 0%

commit v1 on v0

v1 whole, which is shorter than its diff:
```python
import functools

import jax
import jax.numpy as jnp
from jax import lax
from jax.experimental import pallas as pl
from jax.experimental.pallas import tpu as pltpu
from jax.sharding import PartitionSpec as P

MESH = pl.DeviceIdType.MESH
F32 = jnp.float32
BF16 = jnp.bfloat16


def torus_offsets(nx, nz):
    def hops(dx, dz):
        return min(dx, nx - dx) + min(dz, nz - dz)

    every = [(dx, dz) for dx in range(nx) for dz in range(nz) if dx or dz]
    return sorted(every, key=lambda o: -hops(*o))


def dot_nt(a, b):
    return lax.dot_general(a, b, (((1,), (1,)), ((), ())), preferred_element_type=F32)


def dot_nn(a, b):
    return jnp.dot(a, b, preferred_element_type=F32)


def kernel(
    nx,
    nz,
    nn,
    charges,
    leaf_in,
    leaf_out,
    near_list,
    near_blocks,
    leaf_partners,
    leaf_couple,
    leaf_up,
    leaf_down,
    box_partners,
    box_couple,
    box_transfer,
    top_partners,
    top_couple,
    out,
    cwin,
    mpair,
    mwin,
    bs,
    bmd,
    topb,
    li,
    lo,
    nb,
    lc,
    lu,
    ld,
    bc,
    bt,
    tc,
    nl,
    lp,
    bp,
    tp,
    near,
    coup,
    lsem,
    nsem,
    near_ssem,
    near_rsem,
    leaf_ssem,
    leaf_rsem,
    far_ssem,
    far_rsem,
):
    ns = nx * nz
    s = lax.axis_index("leaf")
    n = lax.axis_index("near")
    x = s // nz
    z = s % nz
    far = torus_offsets(nx, nz)
    group = 8 * nn
    ring = 4 * group
    place = [(s + i + 3) % 4 * group + n * 8 for i in range(3)]
    own, own_pair = place[1], place[1] // 2

    local = []

    def load(src, dst, sem):
        cp = pltpu.make_async_copy(src, dst, sem)
        cp.start()
        return cp

    c_ch = load(charges, cwin.at[pl.ds(own, 8)], lsem.at[0])
    c_li = load(leaf_in, li, lsem.at[1])
    c_lu0 = load(leaf_up.at[0], lu.at[pl.ds(0, 64)], lsem.at[2])
    c_lu1 = load(leaf_up.at[0], lu.at[pl.ds(64, 64)], lsem.at[3])
    c_bt = load(box_transfer.at[0], bt, lsem.at[4])

    barrier = pltpu.get_barrier_semaphore()
    for dx, dz in far:
        pl.semaphore_signal(
            barrier, 1, device_id=(((x + dx) % nx) * nz + (z + dz) % nz, n), device_id_type=MESH
        )
    for d in range(1, nn):
        pl.semaphore_signal(barrier, 1, device_id=(s, (n + d) % nn), device_id_type=MESH)

    c_nl = load(near_list, nl, lsem.at[5])
    c_lp = load(leaf_partners, lp, lsem.at[6])
    c_bp = load(box_partners, bp, lsem.at[7])
    c_tp = load(top_partners, tp, lsem.at[8])
    c_bc = load(box_couple.at[0], bc, lsem.at[9])
    c_tc = load(top_couple.at[0], tc, lsem.at[10])
    c_ld = load(leaf_down.at[0], ld, lsem.at[11])
    c_lc = load(leaf_couple, lc, lsem.at[12])
    c_lo = load(leaf_out, lo, lsem.at[13])
    c_nb = [load(near_blocks.at[i], nb.at[i], nsem.at[i]) for i in range(8)]

    low = lax.broadcasted_iota(jnp.int32, (16, 128), 1) < 64

    def pick(a, b):
        return jnp.where(low, a, b)

    c_ch.wait()
    c_li.wait()
    tiles = []
    for t in range(4):
        two = cwin[pl.ds(own + 2 * t, 2)].reshape(32, 128)
        m = dot_nt(two, li[2 * t : 2 * t + 2].reshape(128, 128))
        tile = pick(m[:16], m[16:]).astype(BF16)
        mpair[own_pair + t] = tile
        tiles.append(tile)
    c_lu0.wait()
    c_lu1.wait()
    c_bt.wait()
    box2 = dot_nt(jnp.concatenate(tiles, axis=1), lu[...])
    flipped = pltpu.roll(bt[...].astype(F32), 64, 1).astype(BF16)
    share = dot_nn(box2.astype(BF16)[:, :64], flipped)
    bs[n] = pick(box2, share).astype(BF16)

    pl.semaphore_wait(barrier, len(far) + nn - 1)

    sends = []

    def send(src, dst, ssem, rsem, to):
        cp = pltpu.make_async_remote_copy(
            src_ref=src, dst_ref=dst, send_sem=ssem, recv_sem=rsem, device_id=to, device_id_type=MESH
        )
        cp.start()
        sends.append(cp)
        return cp

    order = sorted(range(1, nn), key=lambda d: -min(d, nn - d))
    r_bs = [
        send(bs.at[n], bs.at[n], near_ssem.at[0, d], near_rsem.at[0, d], (s, (n + d) % nn)) for d in order
    ]
    mine = cwin.at[pl.ds(own, 8)]
    mine_pairs = mpair.at[pl.ds(own_pair, 4)]
    r_ch = [
        send(mine, mine, near_ssem.at[1, d], near_rsem.at[1, d], (s, (n + d) % nn)) for d in order
    ]
    upper = ((s + 1) % ns, n)
    lower = ((s + ns - 1) % ns, n)
    r_ch.append(send(mine, mine, leaf_ssem.at[0], leaf_rsem.at[0], upper))
    r_ch.append(send(mine, mine, leaf_ssem.at[1], leaf_rsem.at[1], lower))
    r_mo = [
        send(mine_pairs, mine_pairs, near_ssem.at[2, d], near_rsem.at[2, d], (s, (n + d) % nn))
        for d in order
    ]
    r_mo.append(send(mine_pairs, mine_pairs, leaf_ssem.at[2], leaf_rsem.at[2], upper))
    r_mo.append(send(mine_pairs, mine_pairs, leaf_ssem.at[3], leaf_rsem.at[3], lower))

    for cp in r_bs:
        cp.wait_recv()
    total = bs[0].astype(F32)
    for i in range(1, nn):
        total = total + bs[i].astype(F32)
    topb[s] = pick(pltpu.roll(total, 64, 1), total).astype(BF16)
    r_far = [
        send(
            topb.at[s],
            topb.at[s],
            far_ssem.at[i],
            far_rsem.at[i],
            (((x + dx) % nx) * nz + (z + dz) % nz, n),
        )
        for i, (dx, dz) in enumerate(far)
    ]

    for i in range(nn):
        b = bs[i].astype(F32)
        bmd[i] = pick(b, pltpu.roll(b, 64, 1)).astype(BF16)
    c_bp.wait()
    c_bc.wait()

    def beside(table, ids):
        return jnp.concatenate([pick(table(ids[2 * t]), table(ids[2 * t + 1])) for t in range(4)], axis=1)

    box_in = beside(lambda i: bmd[i], [bp[0, c] & (nn - 1) for c in range(8)])
    box_part = dot_nt(box_in, bc[...])

    for cp in r_mo:
        cp.wait_recv()

    def spread(q):
        p = mpair[q].astype(F32)
        r = pltpu.roll(p, 64, 1)
        mwin[q, 0] = pick(p, r).astype(BF16)
        mwin[q, 1] = pick(r, p).astype(BF16)

    def spread_own(i, c):
        for j in range(4):
            spread(own_pair - n * 4 + i * 4 + j)
        return c

    lax.fori_loop(0, nn, spread_own, 0)
    for j in range(4):
        spread(place[0] // 2 + j)
        spread(place[2] // 2 + j)
    c_lp.wait()
    c_lc.wait()

    def moment_of(leaf):
        return mwin[(leaf & (ring - 1)) >> 1, leaf & 1]

    for t in range(4):
        rows = [beside(moment_of, [lp[2 * t + h, c] for c in range(8)]) for h in range(2)]
        m = dot_nt(jnp.concatenate(rows, axis=0), lc[2 * t : 2 * t + 2].reshape(128, 512))
        coup[t] = pick(m[:16], m[16:])

    for cp in r_ch:
        cp.wait_recv()
    c_nl.wait()

    def near_leaf(i, c):
        pltpu.make_async_copy(near_blocks.at[i], nb.at[i], nsem.at[i]).wait()
        rows = jnp.concatenate([cwin[nl[i, k] & (ring - 1)] for k in range(27)], axis=1)
        near[i] = dot_nn(rows, nb[i].reshape(27 * 128, 128))
        return c

    lax.fori_loop(0, 8, near_leaf, 0)

    c_tp.wait()
    c_tc.wait()
    c_ld.wait()
    c_lo.wait()
    for cp in r_far:
        cp.wait_recv()
    top_in = beside(lambda i: topb[i], [tp[0, c] & (ns - 1) for c in range(8)])
    top_local = dot_nt(top_in, tc[...]).astype(BF16)
    from_top = dot_nn(top_local, flipped)[:, :64]
    box_local = (box_part + from_top).astype(BF16)
    from_box = dot_nn(box_local, ld[...])
    zero = jnp.zeros((16, 128), F32)
    for t in range(4):
        both = coup[t] + from_box[:, t * 128 : (t + 1) * 128]
        rows = jnp.concatenate([pick(both, zero), pick(zero, both)], axis=0).astype(BF16)
        o = dot_nn(rows, lo[2 * t : 2 * t + 2].reshape(128, 128))
        out[2 * t] = (near[2 * t] + o[:16]).astype(BF16)
        out[2 * t + 1] = (near[2 * t + 1] + o[16:]).astype(BF16)

    for cp in sends:
        cp.wait_send()


def per_device(nx, nz, nn, *args):
    ns = nx * nz
    group = 8 * nn
    n_far = ns - 1
    dma = pltpu.SemaphoreType.DMA
    scratch = [
        pltpu.VMEM((4 * group, 16, 128), BF16),
        pltpu.VMEM((4 * group // 2, 16, 128), BF16),
        pltpu.VMEM((4 * group // 2, 2, 16, 128), BF16),
        pltpu.VMEM((nn, 16, 128), BF16),
        pltpu.VMEM((nn, 16, 128), BF16),
        pltpu.VMEM((ns, 16, 128), BF16),
        pltpu.VMEM((8, 64, 128), BF16),
        pltpu.VMEM((8, 64, 128), BF16),
        pltpu.VMEM((8, 27, 128, 128), BF16),
        pltpu.VMEM((8, 64, 512), BF16),
        pltpu.VMEM((128, 512), BF16),
        pltpu.VMEM((64, 512), BF16),
        pltpu.VMEM((64, 512), BF16),
        pltpu.VMEM((64, 128), BF16),
        pltpu.VMEM((64, 512), BF16),
        pltpu.SMEM((8, 27), jnp.int32),
        pltpu.SMEM((8, 8), jnp.int32),
        pltpu.SMEM((1, 8), jnp.int32),
        pltpu.SMEM((1, 8), jnp.int32),
        pltpu.VMEM((8, 16, 128), F32),
        pltpu.VMEM((4, 16, 128), F32),
        dma((14,)),
        dma((8,)),
        dma((3, nn)),
        dma((3, nn)),
        dma((4,)),
        dma((4,)),
        dma((n_far,)),
        dma((n_far,)),
    ]
    return pl.pallas_call(
        functools.partial(kernel, nx, nz, nn),
        out_shape=jax.ShapeDtypeStruct((8, 16, 128), BF16),
        in_specs=[pl.BlockSpec(memory_space=pltpu.HBM)] * len(args),
        out_specs=pl.BlockSpec(memory_space=pltpu.VMEM),
        scratch_shapes=scratch,
        compiler_params=pltpu.CompilerParams(
            collective_id=0, has_side_effects=True, vmem_limit_bytes=32 * 2**20
        ),
        name="h2_product",
    )(*args)


def solution(mesh):
    ns, nn = mesh.shape["leaf"], mesh.shape["near"]
    nz = 8 if ns % 8 == 0 else ns
    both = ("leaf", "near")
    return jax.shard_map(
        functools.partial(per_device, ns // nz, nz, nn),
        mesh=mesh,
        in_specs=(
            P(both, None, None),
            P(both, None, None),
            P(both, None, None),
            P(both, None),
            P(both, None, None, None),
            P(both, None),
            P(both, None, None),
            P(both, None, None),
            P(both, None, None),
            P(both, None),
            P(both, None, None),
            P(both, None, None),
            P("leaf", None),
            P("leaf", None, None),
        ),
        out_specs=P(both, None, None),
        check_vma=False,
    )
```

time: 169 us -> 38.6 us (0.23)
  blocking collectives: 142 us -> 0 us
  Pallas kernels: 0 us -> 24 us
  matrix products: 10.3 us -> 0 us
  local copies, waits for them, and re-layouts: 6.02 us -> 14 us
  starting transfers between devices: 6.29 us -> 0 us
  other arithmetic: 3.16 us -> 0 us
    all_gather x3 -> x0, blocking collectives: 142 us -> none  [the longest x1 66.6 us: per_device(): lax.all_gather(flat_share, ('leaf', 'near'), axis=0, tiled=True)]
    pallas_call x0 -> x1, Pallas kernels: none -> 24 us  [per_device(): pl.pallas_call(functools.partial(kernel, nx, nz, nn), out_shape=jax.Shape...]
    unnamed x12 -> x29, local copies, waits for them, and re-layouts: 1.07 us -> 14 us
    dot_general x8 -> x0, matrix products: 10.3 us -> none  [the longest x1 4.07 us: per_device(): jnp.einsum('lsrp,lspq->lrq', gathered, near_blocks, preferred_element_typ...]
    ppermute x2 -> x0, starting transfers between devices: 6.29 us -> none  [the longest x1 5 us: padded(): lax.ppermute(tail, axis, [(i, (i + 1) % count) for i in range(ends)])]
    select_n x4 -> x0, other arithmetic: 2.71 us -> none  [the longest x2 1.32 us: side_by_side(): picked = table[partners].reshape(partners.shape[0], rhs_count, rank_width)]
    gather x5 -> x0, local copies, waits for them, and re-layouts: 2.67 us -> none  [the longest x2 1.14 us: side_by_side(): picked = table[partners].reshape(partners.shape[0], rhs_count, rank_width)]
  transfers between devices with their start and end apart: 2 -> 0, of which waited for: 0 -> 0; matrix products, arithmetic and copies ran while one was open for 6% -> 0% of each run, Pallas kernels for 0% -> 0%
where the time goes in v1:
time: 38.6 us; the launch traced here: 38 us
  Pallas kernels  24 us (62%)
  local copies, waits for them, and re-layouts  14 us (36%)
    pallas_call x1, Pallas kernels, per_device(): pl.pallas_call(functools.partial(kernel, nx, nz, nn), out_shape=jax.Shape...  24 us
    unnamed x29, local copies, waits for them, and re-layouts  14 us

profile of v1, /device:TPU:1, one launch (start us, length us, event | category | flops | bytes accessed | tf_op | source)
XLA Modules:
  0.0 38.0 jit_solution(11706778011810216817)
XLA Ops:
  0.0 0.0 copy-start
  0.0 3.0 %copy-done = bf16[8,27,128,128]{3,2,1,0:T(8,128)(2,1)S(1)} copy-done((bf16[8,27,128,128]{3,2,1,0:T(8,128)(2,1)S(1)}, bf16[8,27,128,128]{3,2,1,0:T(8,128)(2,1)}, u32[]{:S(2)}) %copy-start) | copy-done | bytes 7077912
  3.0 0.0 copy-start.1
  3.0 1.0 %copy-done.1 = bf16[8,64,512]{2,1,0:T(8,128)(2,1)S(1)} copy-done((bf16[8,64,512]{2,1,0:T(8,128)(2,1)S(1)}, bf16[8,64,512]{2,1,0:T(8,128)(2,1)}, u32[]{:S(2)}) %copy-start.1) | copy-done | bytes 524312
  4.1 0.0 copy-start.2
  4.1 0.9 %copy-done.2 = bf16[8,64,128]{2,1,0:T(8,128)(2,1)S(1)} copy-done((bf16[8,64,128]{2,1,0:T(8,128)(2,1)S(1)}, bf16[8,64,128]{2,1,0:T(8,128)(2,1)}, u32[]{:S(2)}) %copy-start.2) | copy-done | bytes 131096
  5.0 0.0 copy-start.3
  5.0 0.9 %copy-done.3 = bf16[8,64,128]{2,1,0:T(8,128)(2,1)S(1)} copy-done((bf16[8,64,128]{2,1,0:T(8,128)(2,1)S(1)}, bf16[8,64,128]{2,1,0:T(8,128)(2,1)}, u32[]{:S(2)}) %copy-start.3) | copy-done | bytes 131096
  5.9 0.0 copy-start.4
  5.9 0.8 %copy-done.4 = bf16[1,64,512]{2,1,0:T(8,128)(2,1)S(1)} copy-done((bf16[1,64,512]{2,1,0:T(8,128)(2,1)S(1)}, bf16[1,64,512]{2,1,0:T(8,128)(2,1)}, u32[]{:S(2)}) %copy-start.4) | copy-done | bytes 65560
  6.7 0.0 copy-start.5
  6.7 0.8 %copy-done.5 = bf16[1,64,512]{2,1,0:T(8,128)(2,1)S(1)} copy-done((bf16[1,64,512]{2,1,0:T(8,128)(2,1)S(1)}, bf16[1,64,512]{2,1,0:T(8,128)(2,1)}, u32[]{:S(2)}) %copy-start.5) | copy-done | bytes 65560
  7.5 0.0 copy-start.6
  7.5 0.8 %copy-done.6 = bf16[1,64,512]{2,1,0:T(8,128)(2,1)S(1)} copy-done((bf16[1,64,512]{2,1,0:T(8,128)(2,1)S(1)}, bf16[1,64,512]{2,1,0:T(8,128)(2,1)}, u32[]{:S(2)}) %copy-start.6) | copy-done | bytes 65560
  8.4 0.0 copy-start.7
  8.4 0.8 %copy-done.7 = bf16[1,64,512]{2,1,0:T(8,128)(2,1)S(1)} copy-done((bf16[1,64,512]{2,1,0:T(8,128)(2,1)S(1)}, bf16[1,64,512]{2,1,0:T(8,128)(2,1)}, u32[]{:S(2)}) %copy-start.7) | copy-done | bytes 65560
  9.2 0.8 %copy-done.8 = bf16[8,16,128]{2,1,0:T(8,128)(2,1)S(1)} copy-done((bf16[8,16,128]{2,1,0:T(8,128)(2,1)S(1)}, bf16[8,16,128]{2,1,0:T(8,128)(2,1)}, u32[]{:S(2)}) %copy-start.8) | copy-done | bytes 32792
  10.0 0.7 %copy-done.9 = bf16[1,64,128]{2,1,0:T(8,128)(2,1)S(1)} copy-done((bf16[1,64,128]{2,1,0:T(8,128)(2,1)S(1)}, bf16[1,64,128]{2,1,0:T(8,128)(2,1)}, u32[]{:S(2)}) %copy-start.9) | copy-done | bytes 16408
  10.7 0.7 %copy-done.10 = s32[8,27]{1,0:T(8,128)S(1)} copy-done((s32[8,27]{1,0:T(8,128)S(1)}, s32[8,27]{1,0:T(8,128)}, u32[]{:S(2)}) %copy-start.10) | copy-done | bytes 888
  11.4 0.7 %copy-done.11 = s32[8,8]{1,0:T(8,128)S(1)} copy-done((s32[8,8]{1,0:T(8,128)S(1)}, s32[8,8]{1,0:T(8,128)}, u32[]{:S(2)}) %copy-start.11) | copy-done | bytes 280
  12.1 0.7 %copy-done.12 = s32[1,8]{1,0:T(1,128)S(1)} copy-done((s32[1,8]{1,0:T(1,128)S(1)}, s32[1,8]{1,0:T(1,128)}, u32[]{:S(2)}) %copy-start.12) | copy-done | bytes 56
  12.7 0.7 %copy-done.13 = s32[1,8]{1,0:T(1,128)S(1)} copy-done((s32[1,8]{1,0:T(1,128)S(1)}, s32[1,8]{1,0:T(1,128)}, u32[]{:S(2)}) %copy-start.13) | copy-done | bytes 56
  13.4 24.0 %h2_product.1 = bf16[8,16,128]{2,1,0:T(8,128)(2,1)S(1)} custom-call(bf16[8,16,128]{2,1,0:T(8,128)(2,1)S(1)} %copy-done.8, bf16[8,64,128]{2,1,0:T(8,128)(2,1)S(1)} %copy-done.2, bf16[8,64,128]{2,1,0:T(8,128)(2,1)S(1)} %copy-done.3, s32[8,27]{1,0:T(8,128)S(1)} %copy-done.10, bf16[8,27,128,128]{3,2,1,0:T(8,128)(2,1)S(1)} %copy-done, s32[8,8]{1,0:T(8,128)S(1)} %copy-done.11, ...), custom_call_target="tpu_custom_call" | custom-call | tf_op jit(solution)/shard_map/h2_product/pallas_call | solution.py:306
  37.4 0.6 %copy.16 = bf16[8,16,128]{2,1,0:T(8,128)(2,1)} copy(bf16[8,16,128]{2,1,0:T(8,128)(2,1)S(1)} %h2_product.1) | data formatting | bytes 65536
  (6 shorter events, 0.0 us)
Async XLA Ops:
  0.0 3.0 %copy-start = (bf16[8,27,128,128]{3,2,1,0:T(8,128)(2,1)S(1)}, bf16[8,27,128,128]{3,2,1,0:T(8,128)(2,1)}, u32[]{:S(2)}) copy-start(bf16[8,27,128,128]{3,2,1,0:T(8,128)(2,1)} %near_blocks.1) | copy-start | bytes 21233668
  3.0 1.0 %copy-start.1 = (bf16[8,64,512]{2,1,0:T(8,128)(2,1)S(1)}, bf16[8,64,512]{2,1,0:T(8,128)(2,1)}, u32[]{:S(2)}) copy-start(bf16[8,64,512]{2,1,0:T(8,128)(2,1)} %leaf_couple.1) | copy-start | bytes 1572868
  4.1 0.9 %copy-start.2 = (bf16[8,64,128]{2,1,0:T(8,128)(2,1)S(1)}, bf16[8,64,128]{2,1,0:T(8,128)(2,1)}, u32[]{:S(2)}) copy-start(bf16[8,64,128]{2,1,0:T(8,128)(2,1)} %leaf_in.1) | copy-start | bytes 393220
  5.0 0.9 %copy-start.3 = (bf16[8,64,128]{2,1,0:T(8,128)(2,1)S(1)}, bf16[8,64,128]{2,1,0:T(8,128)(2,1)}, u32[]{:S(2)}) copy-start(bf16[8,64,128]{2,1,0:T(8,128)(2,1)} %leaf_out.1) | copy-start | bytes 393220
  5.9 0.8 %copy-start.4 = (bf16[1,64,512]{2,1,0:T(8,128)(2,1)S(1)}, bf16[1,64,512]{2,1,0:T(8,128)(2,1)}, u32[]{:S(2)}) copy-start(bf16[1,64,512]{2,1,0:T(8,128)(2,1)} %leaf_up.1) | copy-start | bytes 196612
  6.7 0.8 %copy-start.5 = (bf16[1,64,512]{2,1,0:T(8,128)(2,1)S(1)}, bf16[1,64,512]{2,1,0:T(8,128)(2,1)}, u32[]{:S(2)}) copy-start(bf16[1,64,512]{2,1,0:T(8,128)(2,1)} %leaf_down.1) | copy-start | bytes 196612
  7.5 0.8 %copy-start.6 = (bf16[1,64,512]{2,1,0:T(8,128)(2,1)S(1)}, bf16[1,64,512]{2,1,0:T(8,128)(2,1)}, u32[]{:S(2)}) copy-start(bf16[1,64,512]{2,1,0:T(8,128)(2,1)} %box_couple.1) | copy-start | bytes 196612
  8.4 0.8 %copy-start.7 = (bf16[1,64,512]{2,1,0:T(8,128)(2,1)S(1)}, bf16[1,64,512]{2,1,0:T(8,128)(2,1)}, u32[]{:S(2)}) copy-start(bf16[1,64,512]{2,1,0:T(8,128)(2,1)} %top_couple.1) | copy-start | bytes 196612
  9.2 0.8 %copy-start.8 = (bf16[8,16,128]{2,1,0:T(8,128)(2,1)S(1)}, bf16[8,16,128]{2,1,0:T(8,128)(2,1)}, u32[]{:S(2)}) copy-start(bf16[8,16,128]{2,1,0:T(8,128)(2,1)} %charges.1) | copy-start | bytes 98308
  10.0 0.7 %copy-start.9 = (bf16[1,64,128]{2,1,0:T(8,128)(2,1)S(1)}, bf16[1,64,128]{2,1,0:T(8,128)(2,1)}, u32[]{:S(2)}) copy-start(bf16[1,64,128]{2,1,0:T(8,128)(2,1)} %box_transfer.1) | copy-start | bytes 49156
  10.7 0.7 %copy-start.10 = (s32[8,27]{1,0:T(8,128)S(1)}, s32[8,27]{1,0:T(8,128)}, u32[]{:S(2)}) copy-start(s32[8,27]{1,0:T(8,128)} %near_list.1) | copy-start | bytes 2596
  11.4 0.7 %copy-start.11 = (s32[8,8]{1,0:T(8,128)S(1)}, s32[8,8]{1,0:T(8,128)}, u32[]{:S(2)}) copy-start(s32[8,8]{1,0:T(8,128)} %leaf_partners.1) | copy-start | bytes 772
  12.1 0.7 %copy-start.12 = (s32[1,8]{1,0:T(1,128)S(1)}, s32[1,8]{1,0:T(1,128)}, u32[]{:S(2)}) copy-start(s32[1,8]{1,0:T(1,128)} %box_partners.1) | copy-start | bytes 100
  12.7 0.7 %copy-start.13 = (s32[1,8]{1,0:T(1,128)S(1)}, s32[1,8]{1,0:T(1,128)}, u32[]{:S(2)}) copy-start(s32[1,8]{1,0:T(1,128)} %top_partners.1) | copy-start | bytes 100
